TPU v7x, 128 devices: a whole 4x4x4 slice. The times are simulated.
128 devices in a mesh: seq: 32 (over x, z, core), head: 4 (over y).
Axes of the slice: x: 4, y: 4, z: 4, core: 2. Of those that a mesh axis runs over, the one named last changes fastest.
Arguments:
- values: bfloat16 [32768, 8192], P('seq', 'head'), may hold values from -6 to 6
- gate_rows: bfloat16 [32768, 8192], P('seq', 'head')
- input_map: bfloat16 [32768, 1024], P('seq', 'head'), may hold values from -1.5 to 1.5
- output_map: bfloat16 [32768, 1024], P('seq', 'head'), may hold values from -1.5 to 1.5
- decay_rate: bfloat16 [32768, 128], P('seq', 'head')
- step_size: bfloat16 [32768, 128], P('seq', 'head')
- skip_gain: float32 [128], P('head'), may hold values from 0.5 to 1.5
- norm_gain: float32 [8192], P('head'), may hold values from 0.5 to 1.5
- slot_map: int32 [4], replicated, may hold values from 0 to 127, as said below
- state_cache: bfloat16 [128, 128, 64, 256], P(('seq', 'head')), may hold values from -3 to 3
Outputs:
- mixed_rows: bfloat16 [32768, 8192], P('seq', 'head')
- new_cache: bfloat16 [128, 128, 64, 256], P(('seq', 'head'))
Inputs may be any that keep to these rules, and one draw needn't show every extreme that they name: `slot_map`: the slot that receives a head group's final states; groups may share a slot.
All inputs are finite; a program needn't handle non-finite values.
Results may differ from a plain program's by a relative error of at most 0.0014.
The roundings to bfloat16 on the way count: a program that leaves them out, or rounds other values in their place, can miss the bound.
Values may be sent and summed in bfloat16 or wider, within the bound.
A program may use at most 256 MiB of HBM per device.

v0:
```python
import jax
import jax.numpy as jnp
from jax import lax
from jax.sharding import PartitionSpec as P

HEADS = 128
HEAD_DIM = 64
STATE = 256
GROUPS = 4
SPAN = 256


def block_parts(vals, rates, steps, maps_in, maps_out):
    length, heads_here, head_width = vals.shape
    group_count = maps_in.shape[1]
    state_width = maps_in.shape[2]
    per_group = heads_here // group_count
    block_rows = SPAN
    block_count = length // block_rows
    causal = jnp.arange(block_rows)[:, None] >= jnp.arange(block_rows)[None, :]
    vals_blocks = vals.reshape(block_count, block_rows, heads_here, head_width)
    in_blocks = maps_in.reshape(block_count, block_rows, group_count, state_width)
    out_blocks = maps_out.reshape(block_count, block_rows, group_count, state_width)
    steps_blocks = steps.reshape(block_count, block_rows, heads_here)
    running = jnp.cumsum(rates.reshape(block_count, block_rows, heads_here), axis=1)
    inner_prod = jnp.einsum(
        "kign,kjgn->kgij", out_blocks, in_blocks, preferred_element_type=jnp.float32
    )
    running_t = jnp.swapaxes(running, 1, 2)
    spread = running_t[:, :, :, None] - running_t[:, :, None, :]
    pair_decay = jnp.where(causal, jnp.exp(-jnp.where(causal, spread, 0.0)), 0.0)
    weight = inner_prod[:, :, None] * pair_decay.reshape(
        block_count, group_count, per_group, block_rows, block_rows
    )
    weight = weight * jnp.swapaxes(steps_blocks, 1, 2).reshape(
        block_count, group_count, per_group, 1, block_rows
    )
    weight = weight.reshape(block_count, heads_here, block_rows, block_rows).astype(jnp.bfloat16)
    inside = jnp.einsum("khij,kjhp->kihp", weight, vals_blocks, preferred_element_type=jnp.float32)
    trailing = jnp.exp(-(running[:, -1:] - running)) * steps_blocks
    scaled_in = (
        trailing.reshape(block_count, block_rows, group_count, per_group)[..., None]
        * in_blocks[:, :, :, None, :]
    )
    scaled_in = scaled_in.astype(jnp.bfloat16)
    state_add = jnp.einsum(
        "kjgqp,kjgqn->kgqpn",
        vals_blocks.reshape(block_count, block_rows, group_count, per_group, head_width),
        scaled_in,
        preferred_element_type=jnp.float32,
    )
    state_add = state_add.reshape(block_count, heads_here, head_width, state_width)
    return (inside, state_add, running)


def chain_states(state_add, running, start_state):
    block_count, heads_here, head_width, state_width = state_add.shape
    block_total = running[:, -1]
    cum_incl = jnp.cumsum(block_total, axis=0)
    cum_excl = cum_incl - block_total
    ends = jnp.concatenate([cum_excl, cum_incl[-1:]], axis=0)
    earlier = (jnp.arange(block_count + 1)[:, None] > jnp.arange(block_count)[None, :])[:, :, None]
    gap = ends[:, None, :] - cum_incl[None, :, :]
    factor = jnp.where(earlier, jnp.exp(-jnp.where(earlier, gap, 0.0)), 0.0)
    flat_add = state_add.reshape(block_count, heads_here, head_width * state_width)
    summed = jnp.einsum("bch,chx->bhx", factor, flat_add, precision=lax.Precision.HIGHEST)
    summed = summed + jnp.exp(-ends)[:, :, None] * start_state.reshape(
        1, heads_here, head_width * state_width
    )
    summed = summed.reshape(block_count + 1, heads_here, head_width, state_width)
    return (summed[:-1], summed[-1])


def carried_rows(maps_out, entry, running):
    block_count, heads_here, head_width, state_width = entry.shape
    block_rows = SPAN
    group_count = maps_out.shape[1]
    out_blocks = maps_out.reshape(block_count, block_rows, group_count, state_width)
    entry_half = entry.astype(jnp.bfloat16)
    reached = jnp.einsum(
        "kign,kgqn->kigq", out_blocks, entry_half, preferred_element_type=jnp.float32
    )
    return reached * jnp.exp(-running)[..., None]


def shards(
    values,
    gate_rows,
    input_map,
    output_map,
    decay_rate,
    step_size,
    skip_gain,
    norm_gain,
    slot_map,
    state_cache,
):
    tok_local = values.shape[0]
    head_width = HEAD_DIM
    state_width = STATE
    heads_local = values.shape[1] // head_width
    groups_local = input_map.shape[1] // state_width
    per_group = HEADS // GROUPS
    seq_count = lax.axis_size("seq")
    head_count = lax.axis_size("head")
    seq_index = lax.axis_index("seq")
    head_index = lax.axis_index("head")
    heads_each = heads_local // seq_count
    paired = jnp.stack([decay_rate, step_size], axis=2).reshape(tok_local, heads_local * 2)
    moved_values, moved_pairs = (
        lax.all_to_all(values, "seq", split_axis=1, concat_axis=0, tiled=True),
        lax.all_to_all(paired, "seq", split_axis=1, concat_axis=0, tiled=True),
    )
    row_total = moved_values.shape[0]
    moved_pairs = moved_pairs.reshape(row_total, heads_each, 2).astype(jnp.float32)
    maps_in, maps_out = (
        lax.all_gather(input_map, "seq", axis=0, tiled=True),
        lax.all_gather(output_map, "seq", axis=0, tiled=True),
    )
    pick_in = maps_in.reshape(row_total, 1, state_width)
    pick_out = maps_out.reshape(row_total, 1, state_width)
    inside, state_add, running = block_parts(
        moved_values.reshape(row_total, heads_each, head_width),
        moved_pairs[:, :, 0],
        moved_pairs[:, :, 1],
        pick_in,
        pick_out,
    )
    zero_state = jnp.zeros((heads_each, head_width, state_width), jnp.float32)
    entry, last_state = chain_states(state_add, running, zero_state)
    ssd_rows = inside + carried_rows(pick_out, entry, running)
    ssd_half = ssd_rows.astype(jnp.bfloat16).reshape(row_total, heads_each * head_width)
    ssd_local = lax.all_to_all(ssd_half, "seq", split_axis=0, concat_axis=1, tiled=True)
    last_half = last_state.astype(jnp.bfloat16)
    every_state = lax.all_gather(last_half, ("seq", "head"), axis=0, tiled=True)
    every_state = every_state.reshape(seq_count, head_count, heads_each, head_width, state_width)
    every_state = jnp.swapaxes(every_state, 0, 1).reshape(HEADS, head_width, state_width)
    summed = (
        ssd_local.astype(jnp.float32)
        + values.astype(jnp.float32) * jnp.repeat(skip_gain, head_width)[None, :]
    )
    gated = summed * jax.nn.silu(gate_rows.astype(jnp.float32))
    grouped = gated.reshape(tok_local, groups_local, per_group * head_width)
    inverse_rms = lax.rsqrt(jnp.mean(grouped * grouped, axis=2, keepdims=True) + 1e-05)
    mixed_rows = (
        (grouped * inverse_rms).reshape(tok_local, heads_local * head_width) * norm_gain[None, :]
    ).astype(jnp.bfloat16)
    slot_local = state_cache.shape[0]
    device_rank = seq_index * head_count + head_index
    slot_ids = device_rank * slot_local + jnp.arange(slot_local, dtype=jnp.int32)
    head_group = jnp.arange(HEADS, dtype=jnp.int32) // per_group
    group_match = head_group[:, None] == jnp.arange(GROUPS, dtype=jnp.int32)[None, :]
    wanted = jnp.sum(jnp.where(group_match, slot_map[None, :], 0), axis=1)
    matched = slot_ids[:, None] == wanted[None, :]
    new_cache = jnp.where(matched[:, :, None, None], every_state[None], state_cache)
    return (mixed_rows, new_cache)


def solution(mesh):
    return jax.shard_map(
        shards,
        mesh=mesh,
        in_specs=(
            P("seq", "head"),
            P("seq", "head"),
            P("seq", "head"),
            P("seq", "head"),
            P("seq", "head"),
            P("seq", "head"),
            P("head"),
            P("head"),
            P(),
            P(("seq", "head"), None, None, None),
        ),
        out_specs=(P("seq", "head"), P(("seq", "head"), None, None, None)),
        check_vma=False,
    )
```

profile of v0, /device:TPU:33, one launch (start us, length us, event | category | flops | bytes accessed | tf_op | source)
XLA Modules:
  0.0 343.9 jit_solution(9490407032877216288)
XLA Ops:
  7.2 0.0 all-gather.6.cloned.1.call-start
  7.2 0.7 all-gather.6.cloned.1.call-update
  7.9 0.0 all-gather.4.cloned.1.call-start
  7.9 0.7 all-gather.4.cloned.1.call-update
  8.6 0.9 pad_maximum_fusion
  9.5 0.8 copy.105
  10.3 8.3 %all-to-all-start = ((bf16[1024,32,2]{0,2,1:T(2,128)(2,1)}), bf16[1024,32,2]{0,2,1:T(2,128)(2,1)S(1)}, u32[]{:S(2)}, u32[]{:S(2)}) async-start(bf16[1024,32,2]{0,2,1:T(2,128)(2,1)} %copy.105), calls=%async_computation | async-start | bytes 262144 | tf_op jit(solution)/shard_map/all_to_all | solution.py:112
  18.7 6.4 %copy.110 = bf16[1024,2048]{0,1:T(8,128)(2,1)} copy(bf16[1024,2048]{1,0:T(8,128)(2,1)} %param.10) | data formatting | bytes 8388608 | tf_op args[0]
  25.1 0.1 all-to-all-done
  25.3 7.3 %all-to-all-start.1 = ((bf16[1024,32,64]{0,2,1:T(8,128)(2,1)}), bf16[1024,32,64]{0,2,1:T(8,128)(2,1)}, u32[]{:S(2)}, u32[]{:S(2)}) async-start(bf16[1024,32,64]{0,2,1:T(8,128)(2,1)} %bitcast.95), calls=%async_computation.1 | async-start | bytes 8388608 | tf_op jit(solution)/shard_map/all_to_all | solution.py:111
  32.6 0.0 all-gather.8.cloned.1.call-start
  32.7 0.1 convert_element_type.96
  32.8 0.4 fusion.31
  33.2 0.1 copy.106
  33.3 0.1 fusion.33
  33.5 0.1 copy.117
  33.6 0.2 reduce_window_sum.56
  33.8 0.5 slice.42
  34.3 0.1 fusion.32
  34.4 0.1 copy.119
  34.5 0.1 mul.103
  34.6 0.1 copy.114
  34.7 0.1 copy.115
  34.8 0.1 copy.108
  35.0 0.1 copy.122
  35.1 0.7 fusion.26
  35.7 0.7 pad_maximum_fusion.1
  36.4 65.1 %all-to-all-done.1 = bf16[1024,32,64]{0,2,1:T(8,128)(2,1)} async-done(((bf16[1024,32,64]{0,2,1:T(8,128)(2,1)}), bf16[1024,32,64]{0,2,1:T(8,128)(2,1)}, u32[]{:S(2)}, u32[]{:S(2)}) %all-to-all-start.1) | async-done | bytes 4194336 | tf_op jit(solution)/shard_map/all_to_all | solution.py:111
  101.5 6.7 %copy.111 = bf16[32,1024,64]{1,0,2:T(8,128)(2,1)} copy(bf16[32,1024,64]{1,2,0:T(8,128)(2,1)} %bitcast.13) | data formatting | bytes 8388608 | tf_op jit(solution)/shard_map/all_to_all | solution.py:111
  108.3 8.1 %reshape.413 = bf16[128,256,64]{1,0,2:T(8,128)(2,1)} reshape(bf16[32,1024,64]{1,0,2:T(8,128)(2,1)} %copy.111) | data formatting | bytes 8388608 | tf_op jit(solution)/shard_map/reshape.30
  116.4 5.1 %all-gather.6.cloned.1.call-done = bf16[32768,256]{1,0:T(8,128)(2,1)} async-done(((bf16[1024,256]{1,0:T(8,128)(2,1)}), bf16[32768,256]{1,0:T(8,128)(2,1)}) %all-gather.6.cloned.1.call-update) | async-done | bytes 16777232 | tf_op jit(solution)/shard_map/all_gather | solution.py:117
  121.5 10.0 %fusion.3 = f32[128,256,64]{1,2,0:T(8,128)S(1)} fusion(bf16[128,256,256]{2,1,0:T(8,128)(2,1)} %bitcast.97, f32[128,256]{1,0:T(8,128)S(1)} %copy.115, bf16[128,256,64]{1,0,2:T(8,128)(2,1)} %reshape.413), kind=kOutput, calls=%fused_computation.6 | convolution fusion | flops 1098907648 | bytes 29491200 | tf_op jit(solution)/shard_map/kjgqp,kjgqn->kgqpn/dot_general | solution.py:46
  131.6 6.6 %copy.129 = f32[16,8,64,256]{3,1,2,0:T(8,128)S(1)} copy(f32[16,8,64,256]{3,2,1,0:T(8,128)S(1)} %bitcast.94) | data formatting | bytes 16777216
  138.2 9.0 %fusion.2 = bf16[129,1,16384]{2,0,1:T(8,128)(2,1)S(1)} fusion(f32[128,16384]{1,0:T(8,128)S(1)} %bitcast.93, f32[129]{0:T(256)S(1)} %fusion.26, f32[128]{0:T(128)S(1)} %get-tuple-element.19, f32[129]{0:T(256)S(1)} %bitcast.108), kind=kOutput, calls=%fused_computation.5 | convolution fusion | flops 3250700800 | bytes 12617224 | tf_op jit(solution)/shard_map/bch,chx->bhx/dot_general | solution.py:66
  147.2 0.4 slice.43
  147.6 3.3 copy.130
  150.8 0.2 slice_reduce_fusion.1
  151.0 0.6 convert_element_type.93
  151.6 0.0 all-gather.8.cloned.1.call-update
  151.7 45.2 %all-gather.4.cloned.1.call-done = bf16[32768,256]{1,0:T(8,128)(2,1)} async-done(((bf16[1024,256]{1,0:T(8,128)(2,1)}), bf16[32768,256]{1,0:T(8,128)(2,1)}) %all-gather.4.cloned.1.call-update) | async-done | bytes 16777232 | tf_op jit(solution)/shard_map/all_gather | solution.py:118
  196.9 21.4 %fusion.5 = f32[128,256,64]{1,2,0:T(8,128)} fusion(f32[128,256]{1,0:T(8,128)S(1)} %mul.103, f32[128,256]{1,0:T(8,128)S(1)} %copy.108, pred[256,256]{1,0:T(8,128)(4,1)S(1)} %iota_compare_fusion, bf16[128,256,256]{2,1,0:T(8,128)(2,1)} %bitcast.91, bf16[128,256,256]{2,1,0:T(8,128)(2,1)} %bitcast.98, bf16[128,256,64]{1,0,2:T(8,128)(2,1)} %reshape.413), kind=kOutput, calls=%fused_computation.8 | convolution fusion | flops 5427429376 | bytes 46465024 | tf_op jit(solution)/shard_map/khij,kjhp->kihp/dot_general | solution.py:39
  218.3 14.0 %fusion.14 = bf16[128,256,1,64]{1,3,0,2:T(8,128)(2,1)} fusion(f32[128,256,64]{1,2,0:T(8,128)} %fusion.5, f32[128,256]{1,0:T(8,128)S(1)} %copy.122, bf16[128,64,256]{2,1,0:T(8,128)(2,1)} %bitcast.96, bf16[128,256,256]{2,1,0:T(8,128)(2,1)} %bitcast.92), kind=kOutput, calls=%fused_computation.23 | convolution fusion | flops 1080033280 | bytes 33685504 | tf_op jit(solution)/shard_map/kign,kgqn->kigq/dot_general | solution.py:80
  232.3 6.6 %copy.123 = bf16[128,256,1,64]{1,0,3,2:T(8,128)(2,1)} copy(bf16[128,256,1,64]{1,3,0,2:T(8,128)(2,1)} %fusion.14) | data formatting | bytes 8388608 | tf_op jit(solution)/shard_map/convert_element_type | solution.py:132
  238.9 7.5 %all_to_all.34 = bf16[32,1024,64]{1,0,2:T(8,128)(2,1)} reshape(bf16[128,256,1,64]{1,0,3,2:T(8,128)(2,1)} %copy.123) | data formatting | bytes 8388608 | tf_op jit(solution)/shard_map/all_to_all | solution.py:133
  246.5 6.4 %copy.124 = bf16[32,1024,64]{1,2,0:T(8,128)(2,1)} copy(bf16[32,1024,64]{1,0,2:T(8,128)(2,1)} %all_to_all.34) | data formatting | bytes 8388608 | tf_op jit(solution)/shard_map/all_to_all | solution.py:133
  252.9 0.0 copy-start.2
  252.9 0.0 copy-start.3
  252.9 6.3 %all-to-all-start.2 = ((bf16[32,1024,64]{1,2,0:T(8,128)(2,1)}), bf16[32,1024,64]{1,2,0:T(8,128)(2,1)}, u32[]{:S(2)}, u32[]{:S(2)}) async-start(bf16[32,1024,64]{1,2,0:T(8,128)(2,1)} %copy.124), calls=%async_computation.2 | async-start | bytes 8388608 | tf_op jit(solution)/shard_map/all_to_all | solution.py:133
  259.2 6.5 %copy.126 = bf16[1024,2048]{0,1:T(8,128)(2,1)} copy(bf16[1024,2048]{1,0:T(8,128)(2,1)} %param.11) | data formatting | bytes 8388608 | tf_op args[1]
  265.7 0.0 copy-done.2
  265.7 0.1 broadcast_in_dim.60
  265.8 0.1 mul.114
  265.8 0.0 copy-done.3
  265.8 0.1 select_reduce_fusion
  265.9 0.0 copy-start.1
  265.9 49.5 %all-to-all-done.2 = bf16[32,1024,64]{1,2,0:T(8,128)(2,1)} async-done(((bf16[32,1024,64]{1,2,0:T(8,128)(2,1)}), bf16[32,1024,64]{1,2,0:T(8,128)(2,1)}, u32[]{:S(2)}, u32[]{:S(2)}) %all-to-all-start.2) | async-done | bytes 4194336 | tf_op jit(solution)/shard_map/all_to_all | solution.py:133
  315.4 7.0 %multiply_reduce_fusion = (f32[1024]{0:T(1024)S(1)}, f32[1024,2048]{0,1:T(8,128)S(1)}) fusion(bf16[1024,2048]{0,1:T(8,128)(2,1)} %copy.126, f32[2048]{0:T(1024)S(1)} %mul.114, bf16[1024,2048]{0,1:T(8,128)(2,1)} %copy.110, bf16[32,1024,64]{1,2,0:T(8,128)(2,1)} %all-to-all-done.2), kind=kLoop, calls=%fused_computation.22 | loop fusion | flops 25164800 | bytes 20983808 | tf_op jit(solution)/shard_map/reduce_sum | solution.py:144
  322.4 0.0 copy-done.1
  322.4 2.4 multiply_convert_fusion.4
  324.8 6.4 %copy.128 = bf16[1024,2048]{1,0:T(8,128)(2,1)} copy(bf16[1024,2048]{0,1:T(8,128)(2,1)} %multiply_convert_fusion.4) | data formatting | bytes 8388608
  331.3 0.0 all-gather.8.cloned.1.call-done
  331.3 2.7 copy.127
  333.9 0.8 copy-done
  334.7 2.4 broadcast_select_fusion
  (14 shorter events, 0.2 us)
Async XLA Ops:
  7.2 114.3 %all-gather.6.cloned.1.call-start = ((), (), s32[]{:S(2)}) async-start(), calls=%async_computation.4 | async-start | bytes 17301504 | tf_op jit(solution)/shard_map/all_gather | solution.py:117
  7.9 189.0 %all-gather.4.cloned.1.call-start = ((), (), s32[]{:S(2)}) async-start(), calls=%async_computation.3 | async-start | bytes 17301504 | tf_op jit(solution)/shard_map/all_gather | solution.py:118
  10.3 14.9 %all-to-all-start = ((bf16[1024,32,2]{0,2,1:T(2,128)(2,1)}), bf16[1024,32,2]{0,2,1:T(2,128)(2,1)S(1)}, u32[]{:S(2)}, u32[]{:S(2)}) async-start(bf16[1024,32,2]{0,2,1:T(2,128)(2,1)} %copy.105), calls=%async_computation | async-start | bytes 262144 | tf_op jit(solution)/shard_map/all_to_all | solution.py:112
  25.3 76.3 %all-to-all-start.1 = ((bf16[1024,32,64]{0,2,1:T(8,128)(2,1)}), bf16[1024,32,64]{0,2,1:T(8,128)(2,1)}, u32[]{:S(2)}, u32[]{:S(2)}) async-start(bf16[1024,32,64]{0,2,1:T(8,128)(2,1)} %bitcast.95), calls=%async_computation.1 | async-start | bytes 8388608 | tf_op jit(solution)/shard_map/all_to_all | solution.py:111
  32.6 298.7 %all-gather.8.cloned.1.call-start = ((), (), s32[]{:S(2)}) async-start(), calls=%async_computation.5 | async-start | bytes 4227072 | tf_op jit(solution)/shard_map/all_gather | solution.py:135
  252.9 12.8 %copy-start.2 = (f32[32]{0:T(128)S(1)}, f32[32]{0:T(128)}, u32[]{:S(2)}) copy-start(f32[32]{0:T(128)} %param.16) | copy-start | bytes 388
  252.9 13.0 %copy-start.3 = (s32[4]{0:T(128)S(1)}, s32[4]{0:T(128)}, u32[]{:S(2)}) copy-start(s32[4]{0:T(128)} %param.18) | copy-start | bytes 52
  252.9 62.5 %all-to-all-start.2 = ((bf16[32,1024,64]{1,2,0:T(8,128)(2,1)}), bf16[32,1024,64]{1,2,0:T(8,128)(2,1)}, u32[]{:S(2)}, u32[]{:S(2)}) async-start(bf16[32,1024,64]{1,2,0:T(8,128)(2,1)} %copy.124), calls=%async_computation.2 | async-start | bytes 8388608 | tf_op jit(solution)/shard_map/all_to_all | solution.py:133
  265.9 56.5 %copy-start.1 = (f32[2048]{0:T(1024)S(1)}, f32[2048]{0:T(1024)}, u32[]{:S(2)}) copy-start(f32[2048]{0:T(1024)} %param.17) | copy-start | bytes 24580
  331.3 3.4 %copy-start = (bf16[1,128,64,256]{3,2,1,0:T(8,128)(2,1)S(1)}, bf16[1,128,64,256]{3,2,1,0:T(8,128)(2,1)}, u32[]{:S(2)}) copy-start(bf16[1,128,64,256]{3,2,1,0:T(8,128)(2,1)} %param.19) | copy-start | bytes 12582916
Sparse Core Ops, SparseCore 0:
  10.3 111.2 all-gather.5
  123.8 73.0 all-gather.3
  200.1 72.7 all-gather.7
where the time goes:
time: 349 us; the launch traced here: 344 us
  waiting for transfers between devices  166 us (48%)
  local copies, waits for them, and re-layouts  71.8 us (21%)
  matrix products  54.5 us (16%)
  starting transfers between devices  22.1 us (6%)
  other arithmetic  14.8 us (4%)
  between operations  14.2 us (4%)
    all_to_all x1, waiting for transfers between devices, shards(): lax.all_to_all(values, 'seq', split_axis=1, concat_axis=0, tiled=True)  65.1 us
    all_to_all x1, waiting for transfers between devices, shards(): lax.all_to_all(ssd_half, 'seq', split_axis=0, concat_axis=1, tiled=True)  49.5 us
    all_gather x1, waiting for transfers between devices, shards(): lax.all_gather(output_map, 'seq', axis=0, tiled=True)  45.2 us
    unnamed x13, local copies, waits for them, and re-layouts  30 us
    dot_general x1, matrix products, block_parts(): jnp.einsum('khij,kjhp->kihp', weight, vals_blocks, preferred_element_type...  21.4 us
    dot_general x1, matrix products, carried_rows(): jnp.einsum('kign,kgqn->kigq', out_blocks, entry_half, preferred_element_t...  14 us
    all_to_all x2, local copies, waits for them, and re-layouts, shards(): lax.all_to_all(ssd_half, 'seq', split_axis=0, concat_axis=1, tiled=True)  14 us
    dot_general x1, matrix products, block_parts(): jnp.einsum('kjgqp,kjgqn->kgqpn', vals_blocks.reshape(block_count, block_r...  10 us
  transfers between devices with their start and end apart: 6, of which 5 were waited for; matrix products, arithmetic and copies ran while one was open for 37% of the time, Pallas kernels for 0%

commit v1 on v0

v1 whole, which is shorter than its diff:
```python
import functools

import jax
import jax.numpy as jnp
from jax import lax
from jax.experimental import pallas as pl
from jax.experimental.pallas import tpu as pltpu
from jax.sharding import PartitionSpec as P

MESH = pl.DeviceIdType.MESH
F32 = jnp.float32
BF16 = jnp.bfloat16

HEADS = 128
HEAD_DIM = 64
STATE = 256
GROUPS = 4
SPAN = 256
BLOCKS = 4
TOKENS = SPAN * BLOCKS
LOCAL_HEADS = 32
PAIRS = 16
CHIPS = 16
HALF = 128
ROWS = HALF + 8
WIDE = PAIRS * 128
LOG2E = 1.4426950408889634
LAG = 2
EARLY = 9


def dot(a, b):
    return jnp.dot(a, b, preferred_element_type=F32)


def lanes_of(p):
    return pl.ds(pl.multiple_of(p * 128, 128), 128)


def mixer_kernel(
    values, gate, b_ref, c_ref, rates, steps, skip, gain,
    mixed, gath,
    xv, zv, adds, ins, fac, sbuf, prt, cbuf, own_in, ebuf, ent_in, mbuf, pin, entry,
    bt, ip, rcol, run_t, step_t, trail_t, dwide, dec, ddec, sq, ob, fin,
    xsem, zsem, ps_s, ps_r, os_s, os_r, en_s, en_r, ms_s, ms_r,
    gl_s, gz_s, gz_r, gx_s, gx_r, gy_s, gy_r, gp_s, gp_r, out_sem,
):
    seq = lax.axis_index("seq")
    y = lax.axis_index("head")
    c = seq // 2
    k = lax.rem(seq, 2)
    zc = lax.rem(c, 4)
    xc = c // 4
    partner = 2 * c + 1 - k
    first = k == 0

    barrier = pltpu.get_barrier_semaphore()
    pl.semaphore_signal(barrier, inc=1, device_id={"seq": partner}, device_id_type=MESH)

    def greet(i, _):
        peer = lax.rem(c + 1 + i, CHIPS)
        pl.semaphore_signal(barrier, inc=1, device_id={"seq": 2 * peer + k}, device_id_type=MESH)
        return 0

    lax.fori_loop(0, CHIPS - 1, greet, 0)
    for j in range(1, GROUPS):
        pl.semaphore_signal(
            barrier, inc=1, device_id={"head": lax.rem(y + j, GROUPS)}, device_id_type=MESH
        )

    def x_copy(p):
        return pltpu.make_async_copy(values.at[:, lanes_of(p)], xv.at[:, lanes_of(p)], xsem.at[p])

    def start_x(i, _):
        x_copy(lax.rem(c + 1 + i, CHIPS)).start()
        return 0

    lax.fori_loop(0, PAIRS, start_x, 0)
    z_copy = pltpu.make_async_copy(gate, zv, zsem)
    z_copy.start()

    lane = lax.broadcasted_iota(jnp.int32, (SPAN, 128), 1)
    low = lane < 64
    upper = (
        lax.broadcasted_iota(jnp.int32, (SPAN, SPAN), 0)
        <= lax.broadcasted_iota(jnp.int32, (SPAN, SPAN), 1)
    ).astype(BF16)
    low16 = lax.broadcasted_iota(jnp.int32, (PAIRS, 128), 1) < 64
    for b in range(BLOCKS):
        rows = slice(b * SPAN, (b + 1) * SPAN)
        run_b = dot(rates[:, rows], upper) * LOG2E
        step_b = steps[:, rows].astype(F32)
        fill = jnp.zeros((128 - LOCAL_HEADS, SPAN), F32)
        rcol[rows, :] = jnp.concatenate([run_b, fill], axis=0).T
        total = run_b[:, SPAN - 1 : SPAN]
        run_t[:, rows] = run_b
        step_t[:, rows] = step_b
        trail_t[:, rows] = jnp.exp2(run_b - total) * step_b
        dwide[...] = jnp.broadcast_to(jnp.exp2(-total), (LOCAL_HEADS, 128))
        part = jnp.where(low16, dwide[pl.ds(0, PAIRS, 2), :], dwide[pl.ds(1, PAIRS, 2), :])
        dec[b] = part
        ddec[...] = part if b == 0 else ddec[...] * part
        bt[b] = b_ref[rows, :].astype(F32).T
        ip[b] = lax.dot_general(
            c_ref[rows, :], b_ref[rows, :], (((1,), (1,)), ((), ())), preferred_element_type=F32
        )

    pl.semaphore_wait(barrier, 1 + (CHIPS - 1) + (GROUPS - 1))

    def partner_copy(p):
        return pltpu.make_async_remote_copy(
            src_ref=sbuf.at[p, 1 - k], dst_ref=prt.at[p], send_sem=ps_s.at[p], recv_sem=ps_r.at[p],
            device_id={"seq": partner}, device_id_type=MESH,
        )

    def owner_copy(p):
        return pltpu.make_async_remote_copy(
            src_ref=cbuf.at[p], dst_ref=own_in.at[c], send_sem=os_s.at[p], recv_sem=os_r.at[c],
            device_id={"seq": 2 * p + k}, device_id_type=MESH,
        )

    def owner_arrival(j):
        return pltpu.make_async_remote_copy(
            src_ref=cbuf.at[j], dst_ref=own_in.at[j], send_sem=os_s.at[j], recv_sem=os_r.at[j],
            device_id={"seq": 2 * j + k}, device_id_type=MESH,
        )

    def states(p):
        x_copy(p).wait()
        ln = lanes_of(p)
        state = None
        for b in range(BLOCKS):
            rows = slice(b * SPAN, (b + 1) * SPAN)
            x = xv[rows, ln]
            x0 = jnp.where(low, x, jnp.zeros_like(x))
            x1 = jnp.where(low, jnp.zeros_like(x), x)
            wide = bt[b]
            s0 = (wide * trail_t[pl.ds(2 * p, 1), rows]).astype(BF16)
            s1 = (wide * trail_t[pl.ds(2 * p + 1, 1), rows]).astype(BF16)
            add = dot(s0, x0) + dot(s1, x1)
            if b < BLOCKS - 1:
                adds[b, :, ln] = add
            state = add if b == 0 else state * dec[b, pl.ds(p, 1), :] + add
        decay = jnp.broadcast_to(ddec[pl.ds(p, 1), :], (8, 128))
        for h in range(2):
            sbuf[p, h, 0:HALF, :] = state[h * HALF : (h + 1) * HALF]
            sbuf[p, h, HALF:ROWS, :] = decay
        partner_copy(p).start()

    def combine(p):
        partner_copy(p).wait_recv()
        here = sbuf[p, k]
        there = prt[p]
        early = jnp.where(first, here, there)
        late = jnp.where(first, there, here)
        decay = late[HALF : HALF + 1, :]
        return early[0:HALF] * decay + late[0:HALF], early[HALF:ROWS] * late[HALF:ROWS]

    def send_owner(p):
        both, decay = combine(p)
        cbuf[p, 0:HALF, :] = both
        cbuf[p, HALF:ROWS, :] = decay
        owner_copy(p).start()

    def states_step(i, _):
        states(lax.rem(c + 1 + i, CHIPS))

        @pl.when(i >= LAG)
        def _():
            send_owner(lax.rem(c + 1 + i - LAG, CHIPS))

        return 0

    lax.fori_loop(0, PAIRS, states_step, 0)

    def tail_step(i, _):
        send_owner(lax.rem(c + 1 + i, CHIPS))
        return 0

    lax.fori_loop(PAIRS - LAG, PAIRS - 1, tail_step, 0)
    both, decay = combine(c)
    own_in[c, 0:HALF, :] = both
    own_in[c, HALF:ROWS, :] = decay

    tri = (
        lax.broadcasted_iota(jnp.int32, (128, 128), 0)
        >= lax.broadcasted_iota(jnp.int32, (128, 128), 1)
    )

    def inner(p, _):
        ln = lanes_of(p)
        shift = lax.rem(128 - 2 * p, 128)
        for b in range(BLOCKS):
            r0 = b * SPAN
            rows = slice(r0, r0 + SPAN)
            turned = pltpu.roll(rcol[rows, :], shift, 1)
            cols = [jnp.broadcast_to(turned[:, h : h + 1], (SPAN, 128)) for h in range(2)]
            fac[rows, ln] = jnp.exp2(-jnp.where(low, cols[0], cols[1]))
            x = xv[rows, ln]
            top = bottom = None
            for h in range(2):
                xh = jnp.where(low, x, jnp.zeros_like(x)) if h == 0 else jnp.where(low, jnp.zeros_like(x), x)
                ru = run_t[pl.ds(2 * p + h, 1), rows]
                st = step_t[pl.ds(2 * p + h, 1), rows]
                rt = cols[h]
                w00 = jnp.where(tri, jnp.exp2(ru[:, :128] - rt[:128]), 0.0) * ip[b, :128, :128] * st[:, :128]
                w10 = jnp.exp2(ru[:, :128] - rt[128:]) * ip[b, 128:, :128] * st[:, :128]
                w11 = jnp.where(tri, jnp.exp2(ru[:, 128:] - rt[128:]), 0.0) * ip[b, 128:, 128:] * st[:, 128:]
                t = dot(w00.astype(BF16), xh[:128])
                u = dot(jnp.concatenate([w10.astype(BF16), w11.astype(BF16)], axis=1), xh)
                top = t if top is None else top + t
                bottom = u if bottom is None else bottom + u
            ins[r0 : r0 + 128, ln] = top
            ins[r0 + 128 : r0 + 256, ln] = bottom
        return 0

    lax.fori_loop(0, EARLY, inner, 0)

    def scan_step(j, state):
        @pl.when(j != c)
        def _():
            owner_arrival(j).wait_recv()

        ebuf[j] = state
        return state * own_in[j, HALF : HALF + 1, :] + own_in[j, 0:HALF, :]

    last = lax.fori_loop(0, CHIPS, scan_step, jnp.zeros((HALF, 128), F32))
    fin[...] = last.T.astype(BF16)

    def z_send(j):
        to = xc * 4 + lax.rem(zc + j, 4)
        return pltpu.make_async_remote_copy(
            src_ref=fin, dst_ref=gath.at[k, y, c], send_sem=gz_s.at[j - 1], recv_sem=gz_r.at[j - 1],
            device_id={"seq": 2 * to + k}, device_id_type=MESH,
        )

    def z_arrival(j):
        src = xc * 4 + lax.rem(zc + 4 - j, 4)
        return pltpu.make_async_remote_copy(
            src_ref=fin, dst_ref=gath.at[k, y, src], send_sem=gz_s.at[j - 1], recv_sem=gz_r.at[j - 1],
            device_id={"seq": 2 * src + k}, device_id_type=MESH,
        )

    keep = pltpu.make_async_copy(fin, gath.at[k, y, c], gl_s)
    keep.start()
    for j in range(1, 4):
        z_send(j).start()

    def entry_copy(j):
        return pltpu.make_async_remote_copy(
            src_ref=ebuf.at[j], dst_ref=ent_in.at[c], send_sem=en_s.at[j], recv_sem=en_r.at[c],
            device_id={"seq": 2 * j + k}, device_id_type=MESH,
        )

    def entry_arrival(p):
        return pltpu.make_async_remote_copy(
            src_ref=ebuf.at[p], dst_ref=ent_in.at[p], send_sem=en_s.at[p], recv_sem=en_r.at[p],
            device_id={"seq": 2 * p + k}, device_id_type=MESH,
        )

    def send_entry(i, _):
        entry_copy(lax.rem(c + 1 + i, CHIPS)).start()
        return 0

    lax.fori_loop(0, CHIPS - 1, send_entry, 0)
    ent_in[c] = ebuf[c]

    lax.fori_loop(EARLY, PAIRS, inner, 0)

    def x_send(j):
        to = lax.rem(xc + j, 4) * 4 + zc
        return pltpu.make_async_remote_copy(
            src_ref=gath.at[k, y, pl.ds(xc * 4, 4)], dst_ref=gath.at[k, y, pl.ds(xc * 4, 4)],
            send_sem=gx_s.at[j - 1], recv_sem=gx_r.at[j - 1],
            device_id={"seq": 2 * to + k}, device_id_type=MESH,
        )

    def x_arrival(j):
        src = lax.rem(xc + 4 - j, 4)
        return pltpu.make_async_remote_copy(
            src_ref=gath.at[k, y, pl.ds(src * 4, 4)], dst_ref=gath.at[k, y, pl.ds(src * 4, 4)],
            send_sem=gx_s.at[j - 1], recv_sem=gx_r.at[j - 1],
            device_id={"seq": 2 * (src * 4 + zc) + k}, device_id_type=MESH,
        )

    keep.wait()
    for j in range(1, 4):
        z_arrival(j).wait_recv()
    for j in range(1, 4):
        x_send(j).start()

    def entry_to_partner(p):
        return pltpu.make_async_remote_copy(
            src_ref=mbuf.at[p], dst_ref=pin.at[p], send_sem=ms_s.at[p], recv_sem=ms_r.at[p],
            device_id={"seq": partner}, device_id_type=MESH,
        )

    z_copy.wait()
    sq[...] = jnp.zeros_like(sq)

    def receive(p):
        @pl.when(p != c)
        def _():
            entry_arrival(p).wait_recv()

        state = ent_in[p]
        early = jnp.where(first, sbuf[p, 0], prt[p])
        moved = state * early[HALF : HALF + 1, :] + early[0:HALF]
        entry[pl.ds(pl.multiple_of(k * HALF, HALF), HALF), lanes_of(p)] = jnp.where(first, state, moved)
        mbuf[p] = jnp.where(first, moved, state)
        entry_to_partner(p).start()

    def finish(p):
        ln = lanes_of(p)
        entry_to_partner(p).wait_recv()
        entry[pl.ds(pl.multiple_of((1 - k) * HALF, HALF), HALF), ln] = pin[p]
        state = entry[:, ln]
        skip_row = jnp.where(low[0:1], skip[2 * p], skip[2 * p + 1])
        for b in range(BLOCKS):
            rows = slice(b * SPAN, (b + 1) * SPAN)
            carried = dot(c_ref[rows, :], state.astype(BF16))
            ssd = (ins[rows, ln] + carried * fac[rows, ln]).astype(BF16).astype(F32)
            z = zv[rows, ln].astype(F32)
            gated = (ssd + xv[rows, ln].astype(F32) * skip_row) * (z / (1.0 + jnp.exp(-z)))
            ins[rows, ln] = gated
            sq[rows, :] = sq[rows, :] + gated * gated
            if b < BLOCKS - 1:
                state = state * dec[b, pl.ds(p, 1), :] + adds[b, :, ln]

    def finish_step(i, _):
        @pl.when(i < PAIRS)
        def _():
            receive(lax.rem(c + CHIPS - i, CHIPS))

        @pl.when(i >= LAG)
        def _():
            finish(lax.rem(c + CHIPS + LAG - i, CHIPS))

        return 0

    def y_send(j):
        return pltpu.make_async_remote_copy(
            src_ref=gath.at[k, y], dst_ref=gath.at[k, y], send_sem=gy_s.at[j - 1], recv_sem=gy_r.at[j - 1],
            device_id={"head": lax.rem(y + j, 4)}, device_id_type=MESH,
        )

    def y_arrival(j):
        src = lax.rem(y + 4 - j, 4)
        return pltpu.make_async_remote_copy(
            src_ref=gath.at[k, src], dst_ref=gath.at[k, src], send_sem=gy_s.at[j - 1], recv_sem=gy_r.at[j - 1],
            device_id={"head": src}, device_id_type=MESH,
        )

    def p_send(j):
        at = lax.rem(y + 4 - j, 4)
        return pltpu.make_async_remote_copy(
            src_ref=gath.at[k, at], dst_ref=gath.at[k, at], send_sem=gp_s.at[j], recv_sem=gp_r.at[j],
            device_id={"seq": partner}, device_id_type=MESH,
        )

    def p_arrival(j):
        at = lax.rem(y + 4 - j, 4)
        return pltpu.make_async_remote_copy(
            src_ref=gath.at[1 - k, at], dst_ref=gath.at[1 - k, at], send_sem=gp_s.at[j], recv_sem=gp_r.at[j],
            device_id={"seq": partner}, device_id_type=MESH,
        )

    lax.fori_loop(0, 7, finish_step, 0)
    for j in range(1, 4):
        x_arrival(j).wait_recv()
    for j in range(1, 4):
        y_send(j).start()
    p_send(0).start()
    lax.fori_loop(7, PAIRS + LAG, finish_step, 0)

    def out_copy(b):
        rows = pl.ds(b * SPAN, SPAN)
        return pltpu.make_async_copy(ob.at[rows, :], mixed.at[rows, :], out_sem.at[b])

    for b in range(BLOCKS):
        rows = slice(b * SPAN, (b + 1) * SPAN)
        mean = jnp.sum(sq[rows, :], axis=1, keepdims=True) * (1.0 / WIDE)
        inverse = jnp.broadcast_to(lax.rsqrt(mean + 1e-05), (SPAN, 128))

        def norm_step(p, _, rows=rows, inverse=inverse):
            ln = lanes_of(p)
            ob[rows, ln] = (ins[rows, ln] * inverse * gain[pl.ds(p, 1), :]).astype(BF16)
            return 0

        lax.fori_loop(0, PAIRS, norm_step, 0)
        out_copy(b).start()

    for j in (1, 3, 2):
        y_arrival(j).wait_recv()
        p_send(j).start()
    for b in range(BLOCKS):
        out_copy(b).wait()
    for j in range(1, 4):
        z_send(j).wait_send()
        x_send(j).wait_send()
        y_send(j).wait_send()
    for j in range(4):
        p_send(j).wait_send()
        p_arrival(j).wait_recv()

    def drain(p, _):
        partner_copy(p).wait_send()
        entry_to_partner(p).wait_send()

        @pl.when(p != c)
        def _():
            owner_copy(p).wait_send()
            entry_copy(p).wait_send()

        return 0

    lax.fori_loop(0, PAIRS, drain, 0)


def run_mixer(values, gate, input_map, output_map, rates, steps, skip, gain):
    vm = lambda *shape: pltpu.VMEM(shape, F32)
    dma = lambda *shape: pltpu.SemaphoreType.DMA(shape)
    any_spec = pl.BlockSpec(memory_space=pl.ANY)
    vmem_spec = pl.BlockSpec(memory_space=pltpu.VMEM)
    return pl.pallas_call(
        mixer_kernel,
        out_shape=(
            jax.ShapeDtypeStruct((TOKENS, WIDE), BF16),
            jax.ShapeDtypeStruct((2, GROUPS, CHIPS, 128, 128), BF16),
        ),
        in_specs=[any_spec, any_spec] + [vmem_spec] * 4 + [pl.BlockSpec(memory_space=pltpu.SMEM), vmem_spec],
        out_specs=(any_spec, any_spec),
        scratch_shapes=[
            pltpu.VMEM((TOKENS, WIDE), BF16),
            pltpu.VMEM((TOKENS, WIDE), BF16),
            vm(BLOCKS - 1, STATE, WIDE),
            vm(TOKENS, WIDE),
            vm(TOKENS, WIDE),
            vm(PAIRS, 2, ROWS, 128),
            vm(PAIRS, ROWS, 128),
            vm(PAIRS, ROWS, 128),
            vm(CHIPS, ROWS, 128),
            vm(CHIPS, HALF, 128),
            vm(PAIRS, HALF, 128),
            vm(PAIRS, HALF, 128),
            vm(PAIRS, HALF, 128),
            vm(STATE, WIDE),
            vm(BLOCKS, STATE, SPAN),
            vm(BLOCKS, SPAN, SPAN),
            vm(TOKENS, 128),
            vm(LOCAL_HEADS, TOKENS),
            vm(LOCAL_HEADS, TOKENS),
            vm(LOCAL_HEADS, TOKENS),
            vm(LOCAL_HEADS, 128),
            vm(BLOCKS, PAIRS, 128),
            vm(PAIRS, 128),
            vm(TOKENS, 128),
            pltpu.VMEM((TOKENS, WIDE), BF16),
            pltpu.VMEM((128, HALF), BF16),
            dma(PAIRS), pltpu.SemaphoreType.DMA,
            dma(PAIRS), dma(PAIRS),
            dma(PAIRS), dma(PAIRS),
            dma(PAIRS), dma(PAIRS),
            dma(PAIRS), dma(PAIRS),
            pltpu.SemaphoreType.DMA,
            dma(3), dma(3), dma(3), dma(3), dma(3), dma(3), dma(4), dma(4),
            dma(BLOCKS),
        ],
        compiler_params=pltpu.CompilerParams(
            collective_id=0, has_side_effects=True, vmem_limit_bytes=60 * 1024 * 1024
        ),
        cost_estimate=pl.CostEstimate(flops=6_000_000_000, bytes_accessed=24_000_000, transcendentals=12_000_000),
        name="mixer",
    )(values, gate, input_map, output_map, rates, steps, skip, gain)


def place_kernel(slot_map, cache, gath, rows_in, out, rows_out, cbuf, rbuf, cin, cout, rin, rout):
    rank = lax.axis_index("seq") * GROUPS + lax.axis_index("head")

    def rows_step(b, start):
        rows = pl.ds(b * SPAN, SPAN)
        if start:
            return pltpu.make_async_copy(rows_in.at[rows], rbuf.at[rows], rin.at[b])
        return pltpu.make_async_copy(rbuf.at[rows], rows_out.at[rows], rout.at[b])

    def cache_in(g, h):
        part = pl.ds(h * 8, 8)
        return pltpu.make_async_copy(cache.at[g, part], cbuf.at[g, part], cin.at[2 * g + h])

    def cache_out(g, h):
        part = pl.ds(h * 8, 8)
        return pltpu.make_async_copy(cbuf.at[g, part], out.at[g, part], cout.at[2 * g + h])

    for g in range(GROUPS):
        hit = slot_map[g] == rank

        @pl.when(hit)
        def _(g=g):
            for h in range(2):
                pltpu.make_async_copy(
                    gath.at[h, g], cbuf.at[g, :, :, pl.ds(h * HALF, HALF)], cin.at[2 * g + h]
                ).start()

        @pl.when(jnp.logical_not(hit))
        def _(g=g):
            for h in range(2):
                cache_in(g, h).start()

        rows_step(g, True).start()

    for g in range(GROUPS):
        for h in range(2):
            cache_in(g, h).wait()
        for h in range(2):
            cache_out(g, h).start()
        rows_step(g, True).wait()
        rows_step(g, False).start()
    for g in range(GROUPS):
        for h in range(2):
            cache_out(g, h).wait()
        rows_step(g, False).wait()


def run_place(slot_map, cache, gath, rows):
    any_spec = pl.BlockSpec(memory_space=pl.ANY)
    return pl.pallas_call(
        place_kernel,
        out_shape=(
            jax.ShapeDtypeStruct((GROUPS, PAIRS, 128, STATE), BF16),
            jax.ShapeDtypeStruct((TOKENS, WIDE), BF16),
        ),
        in_specs=[pl.BlockSpec(memory_space=pltpu.SMEM), any_spec, any_spec, any_spec],
        out_specs=(any_spec, any_spec),
        scratch_shapes=[
            pltpu.VMEM((GROUPS, PAIRS, 128, STATE), BF16),
            pltpu.VMEM((TOKENS, WIDE), BF16),
            pltpu.SemaphoreType.DMA((2 * GROUPS,)),
            pltpu.SemaphoreType.DMA((2 * GROUPS,)),
            pltpu.SemaphoreType.DMA((BLOCKS,)),
            pltpu.SemaphoreType.DMA((BLOCKS,)),
        ],
        compiler_params=pltpu.CompilerParams(vmem_limit_bytes=60 * 1024 * 1024),
        name="place",
    )(slot_map, cache, gath, rows)


def shards(
    values, gate_rows, input_map, output_map, decay_rate, step_size, skip_gain, norm_gain, slot_map, state_cache
):
    gain = norm_gain.reshape(PAIRS, 128)
    rows, gath = run_mixer(
        values, gate_rows, input_map, output_map, decay_rate.T, step_size.T, skip_gain, gain
    )
    cache = state_cache.reshape(GROUPS, PAIRS, 128, STATE)
    new_cache, mixed_rows = run_place(slot_map, cache, gath, rows)
    return mixed_rows, new_cache.reshape(state_cache.shape)


def solution(mesh):
    return jax.shard_map(
        shards,
        mesh=mesh,
        in_specs=(
            P("seq", "head"),
            P("seq", "head"),
            P("seq", "head"),
            P("seq", "head"),
            P("seq", "head"),
            P("seq", "head"),
            P("head"),
            P("head"),
            P(),
            P(("seq", "head"), None, None, None),
        ),
        out_specs=(P("seq", "head"), P(("seq", "head"), None, None, None)),
        check_vma=False,
    )
```

time: 349 us -> 89.2 us (0.26)
  the two profiles are of different devices: /device:TPU:33 before, /device:TPU:1 now
where the time goes in v1:
time: 89.2 us; the launch traced here: 89 us
  Pallas kernels  88.4 us (99%)
    pallas_call x1, Pallas kernels, run_mixer(): pl.pallas_call(mixer_kernel, out_shape=(jax.ShapeDtypeStruct((TOKENS, WID...  81.4 us
    pallas_call x1, Pallas kernels, run_place(): pl.pallas_call(place_kernel, out_shape=(jax.ShapeDtypeStruct((GROUPS, PAI...  6.97 us

profile of v1, /device:TPU:1, one launch (start us, length us, event | category | flops | bytes accessed | tf_op | source)
XLA Modules:
  0.0 89.0 jit_solution(15203907634280840369)
XLA Ops:
  0.6 81.4 %mixer.1 = (bf16[1024,2048]{1,0:T(8,128)(2,1)}, bf16[2,4,16,128,128]{4,3,2,1,0:T(8,128)(2,1)}) custom-call(bf16[1024,2048]{1,0:T(8,128)(2,1)} %values.1, bf16[1024,2048]{1,0:T(8,128)(2,1)} %gate.1, bf16[1024,256]{1,0:T(8,128)(2,1)} %b_ref.1, bf16[1024,256]{1,0:T(8,128)(2,1)} %c_ref.1, bf16[32,1024]{1,0:T(8,128)(2,1)} %bitcast.7, bf16[32,1024]{1,0:T(8,128)(2,1)} %bitcast.8, ...), custom_call_target="tpu_custom_call" | custom-call | flops 6000000000 | bytes 24000000 | tf_op jit(solution)/shard_map/mixer/pallas_call | solution.py:425
  82.0 7.0 %place.1 = (bf16[4,16,128,256]{3,2,1,0:T(8,128)(2,1)}, bf16[1024,2048]{1,0:T(8,128)(2,1)}) custom-call(s32[4]{0:T(128)} %slot_map.1, bf16[4,16,128,256]{3,2,1,0:T(8,128)(2,1)} %bitcast.5, bf16[2,4,16,128,128]{4,3,2,1,0:T(8,128)(2,1)} %get-tuple-element.6.gath, bf16[1024,2048]{1,0:T(8,128)(2,1)} %get-tuple-element.7.rows_in), custom_call_target="tpu_custom_call" | custom-call | tf_op jit(solution)/shard_map/place/pallas_call | solution.py:526

commit v2 on v1

v2 whole, which is shorter than its diff:
```python
import functools

import jax
import jax.numpy as jnp
from jax import lax
from jax.experimental import pallas as pl
from jax.experimental.pallas import tpu as pltpu
from jax.sharding import PartitionSpec as P

MESH = pl.DeviceIdType.MESH
F32 = jnp.float32
BF16 = jnp.bfloat16

HEADS = 128
HEAD_DIM = 64
STATE = 256
GROUPS = 4
SPAN = 256
BLOCKS = 4
TOKENS = SPAN * BLOCKS
LOCAL_HEADS = 32
PAIRS = 16
CHIPS = 16
HALF = 128
ROWS = HALF + 8
WIDE = PAIRS * 128
LOG2E = 1.4426950408889634
LAG = 3
TOP = 127.9999
EARLY = 4
MIDDLE = 1
SWITCH = 3
PASS = 14
CUT_B, CUT_C = 96, 112


def dot(a, b):
    return jnp.dot(a, b, preferred_element_type=F32)


def lanes_of(p):
    return pl.ds(pl.multiple_of(p * 128, 128), 128)


ROUTE = (
    (2, 2), (1, 2), (2, 1), (3, 2), (2, 3), (1, 1), (3, 3), (1, 3), (3, 1),
    (2, 0), (0, 2), (1, 0), (0, 1), (3, 0), (0, 3), (0, 0),
)


def pick_step(i, which):
    step = ROUTE[0][which]
    for j in range(1, len(ROUTE)):
        step = jnp.where(i == j, ROUTE[j][which], step)
    return step


def mixer_kernel(
    values, gate, b_ref, c_ref, rates, steps, skip, gain, cache,
    ob, held, ga, gb, gc,
    xv, zv, adds, ins, fac, sbuf, prt, cbuf, own_in, ebuf, ent_in, mbuf, pin, entry,
    bt, ip, rcol, minus, wtop, wlow, run_t, step_t, trail_t, dwide, dec, ddec, sq, fin,
    xsem, zsem, ps_s, ps_r, os_s, os_r, en_s, en_r, ms_s, ms_r,
    gl_s, g1_s, g1_r, g2_s, g2_r, g3_s, g3_r, gh_s, gh_r, gp_s, gp_r, held_sem,
):
    seq = lax.axis_index("seq")
    y = lax.axis_index("head")
    c = seq // 2
    k = lax.rem(seq, 2)
    zc = lax.rem(c, 4)
    xc = c // 4
    partner = 2 * c + 1 - k

    def served(i):
        return lax.rem(xc + pick_step(i, 0), 4) * 4 + lax.rem(zc + pick_step(i, 1), 4)

    def serving(i):
        return lax.rem(xc + 4 - pick_step(i, 0), 4) * 4 + lax.rem(zc + 4 - pick_step(i, 1), 4)

    first = k == 0

    barrier = pltpu.get_barrier_semaphore()
    pl.semaphore_signal(barrier, inc=1, device_id={"seq": partner}, device_id_type=MESH)

    def greet(i, _):
        peer = lax.rem(c + 1 + i, CHIPS)
        pl.semaphore_signal(barrier, inc=1, device_id={"seq": 2 * peer + k}, device_id_type=MESH)
        return 0

    lax.fori_loop(0, CHIPS - 1, greet, 0)
    for j in range(1, GROUPS):
        pl.semaphore_signal(
            barrier, inc=1, device_id={"head": lax.rem(y + j, GROUPS)}, device_id_type=MESH
        )

    def x_copy(p):
        return pltpu.make_async_copy(values.at[:, lanes_of(p)], xv.at[:, lanes_of(p)], xsem.at[p])

    def start_x(i, _):
        x_copy(served(i)).start()
        return 0

    lax.fori_loop(0, PAIRS, start_x, 0)
    z_copy = pltpu.make_async_copy(gate, zv, zsem)
    z_copy.start()
    held_copy = pltpu.make_async_copy(cache, held, held_sem)
    held_copy.start()

    lane = lax.broadcasted_iota(jnp.int32, (SPAN, 128), 1)
    low = lane < 64
    upper = (
        lax.broadcasted_iota(jnp.int32, (SPAN, SPAN), 0)
        <= lax.broadcasted_iota(jnp.int32, (SPAN, SPAN), 1)
    ).astype(BF16)
    causal = (
        lax.broadcasted_iota(jnp.int32, (SPAN, SPAN), 0)
        >= lax.broadcasted_iota(jnp.int32, (SPAN, SPAN), 1)
    )
    low16 = lax.broadcasted_iota(jnp.int32, (PAIRS, 128), 1) < 64
    for b in range(BLOCKS):
        rows = slice(b * SPAN, (b + 1) * SPAN)
        run_b = dot(rates[:, rows], upper) * LOG2E
        step_b = steps[:, rows].astype(F32)
        parts, rest = [], -run_b
        for _ in range(3):
            parts.append(rest.astype(BF16).astype(F32))
            rest = rest - parts[-1]
        parts.append(jnp.zeros((128 - 3 * LOCAL_HEADS, SPAN), F32))
        rcol[rows, :] = jnp.concatenate(parts, axis=0).T.astype(BF16)
        total = run_b[:, SPAN - 1 : SPAN]
        run_t[:, rows] = run_b
        step_t[:, rows] = step_b
        trail_t[:, rows] = jnp.exp2(run_b - total) * step_b
        dwide[...] = jnp.broadcast_to(jnp.exp2(-total), (LOCAL_HEADS, 128))
        part = jnp.where(low16, dwide[pl.ds(0, PAIRS, 2), :], dwide[pl.ds(1, PAIRS, 2), :])
        dec[b] = part
        ddec[...] = part if b == 0 else ddec[...] * part
        bt[b] = b_ref[rows, :].astype(F32).T
        inner_prod = lax.dot_general(
            c_ref[rows, :], b_ref[rows, :], (((1,), (1,)), ((), ())), preferred_element_type=F32
        )
        ip[b] = jnp.where(causal, inner_prod, 0.0)

    def partner_copy(p):
        return pltpu.make_async_remote_copy(
            src_ref=sbuf.at[p, 1 - k], dst_ref=prt.at[p], send_sem=ps_s.at[p], recv_sem=ps_r.at[p],
            device_id={"seq": partner}, device_id_type=MESH,
        )

    def owner_copy(p):
        return pltpu.make_async_remote_copy(
            src_ref=cbuf.at[p], dst_ref=own_in.at[c], send_sem=os_s.at[p], recv_sem=os_r.at[c],
            device_id={"seq": 2 * p + k}, device_id_type=MESH,
        )

    def owner_arrival(j):
        return pltpu.make_async_remote_copy(
            src_ref=cbuf.at[j], dst_ref=own_in.at[j], send_sem=os_s.at[j], recv_sem=os_r.at[j],
            device_id={"seq": 2 * j + k}, device_id_type=MESH,
        )

    def states(p):
        ln = lanes_of(p)
        state = None
        for b in range(BLOCKS):
            rows = slice(b * SPAN, (b + 1) * SPAN)
            x = xv[rows, ln]
            wide = bt[b]
            s0 = (wide * trail_t[pl.ds(2 * p, 1), rows]).astype(BF16)
            s1 = (wide * trail_t[pl.ds(2 * p + 1, 1), rows]).astype(BF16)
            add = jnp.where(low, dot(s0, x), dot(s1, x))
            if b < BLOCKS - 1:
                adds[b, :, ln] = add
            state = add if b == 0 else state * dec[b, pl.ds(p, 1), :] + add
        decay = jnp.broadcast_to(ddec[pl.ds(p, 1), :], (8, 128))
        for h in range(2):
            sbuf[p, h, 0:HALF, :] = state[h * HALF : (h + 1) * HALF]
            sbuf[p, h, HALF:ROWS, :] = decay

    def combine(p):
        partner_copy(p).wait_recv()
        here = sbuf[p, k]
        there = prt[p]
        early = jnp.where(first, here, there)
        late = jnp.where(first, there, here)
        decay = late[HALF : HALF + 1, :]
        return early[0:HALF] * decay + late[0:HALF], early[HALF:ROWS] * late[HALF:ROWS]

    def send_owner(p):
        both, decay = combine(p)
        cbuf[p, 0:HALF, :] = both
        cbuf[p, HALF:ROWS, :] = decay
        owner_copy(p).start()

    def states_step(i, _):
        first_p, second_p = served(2 * i), served(2 * i + 1)
        x_copy(first_p).wait()
        x_copy(second_p).wait()
        states(first_p)
        states(second_p)

        @pl.when(i == 0)
        def _():
            pl.semaphore_wait(barrier, 1 + (CHIPS - 1) + (GROUPS - 1))

        partner_copy(first_p).start()
        partner_copy(second_p).start()

        @pl.when(i >= 1)
        def _():
            send_owner(served(2 * i - 2))
            send_owner(served(2 * i - 1))

        return 0

    lax.fori_loop(0, PAIRS // 2, states_step, 0)
    send_owner(served(PAIRS - 2))
    both, decay = combine(c)
    own_in[c, 0:HALF, :] = both
    own_in[c, HALF:ROWS, :] = decay

    row_s = lax.rem(lax.broadcasted_iota(jnp.int32, (128, 256), 0), LOCAL_HEADS)
    lane_s = lax.broadcasted_iota(jnp.int32, (128, 256), 1) // 128
    head_s = row_s - lane_s

    def spread(p, slot):
        pick = jnp.where(head_s == 2 * p, 1.0, 0.0).astype(BF16)
        for b in range(BLOCKS):
            rows = slice(b * SPAN, (b + 1) * SPAN)
            minus[slot, rows, :] = dot(rcol[rows, :], pick)

    def weigh(p, slot, b):
        ln = lanes_of(p)
        r0 = b * SPAN
        rows = slice(r0, r0 + SPAN)
        m = [minus[slot, rows, 128 * h : 128 * h + 128] for h in range(2)]
        fac[rows, ln] = jnp.exp2(jnp.where(low, m[0], m[1]))
        for h in range(2):
            ru = run_t[pl.ds(2 * p + h, 1), rows]
            st = step_t[pl.ds(2 * p + h, 1), rows]
            near = slice(128 * h, 128 * h + 128)
            w00 = jnp.exp2(jnp.minimum(ru[:, :128] + m[h][:128], TOP)) * ip[b, :128, :128] * st[:, :128]
            wtop[slot, b, near, :] = w00.astype(BF16)
            w10 = jnp.exp2(ru[:, :128] + m[h][128:]) * ip[b, 128:, :128] * st[:, :128]
            wlow[slot, b, near, 0:128] = w10.astype(BF16)
            w11 = jnp.exp2(jnp.minimum(ru[:, 128:] + m[h][128:], TOP)) * ip[b, 128:, 128:] * st[:, 128:]
            wlow[slot, b, near, 128:256] = w11.astype(BF16)

    def apply(p, slot, b):
        ln = lanes_of(p)
        r0 = b * SPAN
        x = xv[r0 : r0 + SPAN, ln]
        top = dot(wtop[slot, b], x[:128])
        bottom = dot(wlow[slot, b], x)
        ins[r0 : r0 + 128, ln] = jnp.where(low[:128], top[:128], top[128:])
        ins[r0 + 128 : r0 + 256, ln] = jnp.where(low[:128], bottom[:128], bottom[128:])

    def inner(i, _):
        p0, p1 = 2 * i, 2 * i + 1
        old = lax.rem(p1 + PAIRS - 2, PAIRS)
        for b in range(BLOCKS):
            apply(old, 1, b)
            weigh(p0, 0, b)
        spread(lax.rem(p0 + 2, PAIRS), 0)
        for b in range(BLOCKS):
            apply(p0, 0, b)
            weigh(p1, 1, b)
        spread(lax.rem(p1 + 2, PAIRS), 1)
        return 0

    wtop[1] = jnp.zeros_like(wtop[1])
    wlow[1] = jnp.zeros_like(wlow[1])
    spread(0, 0)
    spread(1, 1)
    lax.fori_loop(0, EARLY, inner, 0)

    def scan_step(j, state):
        @pl.when(j != c)
        def _():
            owner_arrival(j).wait_recv()

        ebuf[j] = state
        return state * own_in[j, HALF : HALF + 1, :] + own_in[j, 0:HALF, :]

    last = lax.fori_loop(0, CHIPS, scan_step, jnp.zeros((HALF, 128), F32))
    fin[...] = last.T.astype(BF16)

    rows_a, rows_b, rows_c = pl.ds(0, CUT_B), pl.ds(CUT_B, CUT_C - CUT_B), pl.ds(CUT_C, 128 - CUT_C)
    parts = ((rows_a, ga, "zxy"), (rows_b, gb, "yzx"), (rows_c, gc, "yxz"))

    def keep(n):
        rows, g, _ = parts[n]
        return pltpu.make_async_copy(fin.at[rows], g.at[k, y, xc, zc], gl_s.at[n])

    def peer(axis, j):
        if axis == "y":
            return {"head": lax.rem(y + j, 4)}
        if axis == "x":
            return {"seq": 2 * (lax.rem(xc + j, 4) * 4 + zc) + k}
        return {"seq": 2 * (xc * 4 + lax.rem(zc + j, 4)) + k}

    def region(g, done, axis, j):
        at = {"y": y, "x": xc, "z": zc}
        if j:
            at[axis] = lax.rem(at[axis] + 4 - j, 4)
        index = [k] + [slice(None) if a in done else at[a] for a in "yxz"]
        return g.at[tuple(index)]

    def stage_copy(n, stage, j, arrival):
        rows, g, order = parts[n]
        axis = order[stage]
        there = region(g, order[:stage], axis, j if arrival else 0)
        source = fin.at[rows] if stage == 0 else there
        sem_s, sem_r = ((g1_s, g1_r), (g2_s, g2_r), (g3_s, g3_r))[stage]
        return pltpu.make_async_remote_copy(
            src_ref=source, dst_ref=there, send_sem=sem_s.at[n, j - 1], recv_sem=sem_r.at[n, j - 1],
            device_id=peer(axis, j), device_id_type=MESH,
        )

    def stage_send(n, stage):
        for j in (1, 3, 2):
            stage_copy(n, stage, j, False).start()

    def stage_arrive(n, stage):
        for j in (1, 3, 2):
            stage_copy(n, stage, j, True).wait_recv()

    def pass_on(j, arrival):
        half = pl.ds(0, 2) if j == 1 else pl.ds(2, 2)
        at = lax.rem(y + (2 if arrival else 4 - j), 4)
        part = ga.at[k, at, half]
        return pltpu.make_async_remote_copy(
            src_ref=part, dst_ref=part, send_sem=gh_s.at[j // 2], recv_sem=gh_r.at[j // 2],
            device_id=peer("y", j), device_id_type=MESH,
        )

    for n in range(3):
        keep(n).start()
    for n in range(3):
        stage_send(n, 0)

    def entry_copy(j):
        return pltpu.make_async_remote_copy(
            src_ref=ebuf.at[j], dst_ref=ent_in.at[c], send_sem=en_s.at[j], recv_sem=en_r.at[c],
            device_id={"seq": 2 * j + k}, device_id_type=MESH,
        )

    def entry_arrival(p):
        return pltpu.make_async_remote_copy(
            src_ref=ebuf.at[p], dst_ref=ent_in.at[p], send_sem=en_s.at[p], recv_sem=en_r.at[p],
            device_id={"seq": 2 * p + k}, device_id_type=MESH,
        )

    def send_entry(i, _):
        entry_copy(served(i)).start()
        return 0

    lax.fori_loop(EARLY, EARLY + MIDDLE, inner, 0)
    for n in range(3):
        keep(n).wait()
        stage_arrive(n, 0)
        stage_send(n, 1)
    lax.fori_loop(0, CHIPS - 1, send_entry, 0)
    ent_in[c] = ebuf[c]

    lax.fori_loop(EARLY + MIDDLE, PAIRS // 2, inner, 0)
    for b in range(BLOCKS):
        apply(PAIRS - 1, 1, b)

    def entry_to_partner(p):
        return pltpu.make_async_remote_copy(
            src_ref=mbuf.at[p], dst_ref=pin.at[p], send_sem=ms_s.at[p], recv_sem=ms_r.at[p],
            device_id={"seq": partner}, device_id_type=MESH,
        )

    z_copy.wait()
    sq[...] = jnp.zeros_like(sq)

    def receive(p):
        @pl.when(p != c)
        def _():
            entry_arrival(p).wait_recv()

        state = ent_in[p]
        early = jnp.where(first, sbuf[p, 0], prt[p])
        moved = state * early[HALF : HALF + 1, :] + early[0:HALF]
        entry[pl.ds(pl.multiple_of(k * HALF, HALF), HALF), lanes_of(p)] = jnp.where(first, state, moved)
        mbuf[p] = jnp.where(first, moved, state)
        entry_to_partner(p).start()

    def finish(p):
        ln = lanes_of(p)
        entry_to_partner(p).wait_recv()
        entry[pl.ds(pl.multiple_of((1 - k) * HALF, HALF), HALF), ln] = pin[p]
        state = entry[:, ln]
        skip_row = jnp.where(low[0:1], skip[2 * p], skip[2 * p + 1])
        for b in range(BLOCKS):
            rows = slice(b * SPAN, (b + 1) * SPAN)
            carried = dot(c_ref[rows, :], state.astype(BF16))
            ssd = (ins[rows, ln] + carried * fac[rows, ln]).astype(BF16).astype(F32)
            z = zv[rows, ln].astype(F32)
            half_z = z * 0.5
            gated = (ssd + xv[rows, ln].astype(F32) * skip_row) * (half_z + half_z * jnp.tanh(half_z))
            ins[rows, ln] = gated
            sq[rows, :] = sq[rows, :] + gated * gated
            if b < BLOCKS - 1:
                state = state * dec[b, pl.ds(p, 1), :] + adds[b, :, ln]

    def finish_step(i, _):
        @pl.when(i < PAIRS)
        def _():
            receive(serving(lax.rem(i + PAIRS - 1, PAIRS)))

        @pl.when(i >= LAG)
        def _():
            finish(serving(lax.rem(i + PAIRS - 1 - LAG, PAIRS)))

        return 0

    def to_partner(n, at, half):
        g = parts[n][1]
        if n == 0:
            return g.at[half, at]
        return g.at[half]

    def p_copy(i, arrival):
        n = 0 if i < 4 else i - 3
        at = lax.rem(y + 4 - i, 4)
        part = to_partner(n, at, 1 - k if arrival else k)
        return pltpu.make_async_remote_copy(
            src_ref=part, dst_ref=part, send_sem=gp_s.at[i], recv_sem=gp_r.at[i],
            device_id={"seq": partner}, device_id_type=MESH,
        )

    lax.fori_loop(0, SWITCH, finish_step, 0)
    stage_arrive(0, 1)
    for j in (1, 3):
        stage_copy(0, 2, j, False).start()
    for n in (1, 2):
        stage_arrive(n, 1)
        stage_send(n, 2)
    p_copy(0, False).start()
    lax.fori_loop(SWITCH, PASS, finish_step, 0)
    for j in (1, 3):
        stage_copy(0, 2, j, True).wait_recv()
        pass_on(j, False).start()
        p_copy(j, False).start()
    lax.fori_loop(PASS, PAIRS + LAG, finish_step, 0)

    for b in range(BLOCKS):
        rows = slice(b * SPAN, (b + 1) * SPAN)
        mean = jnp.sum(sq[rows, :], axis=1, keepdims=True) * (1.0 / WIDE)
        inverse = jnp.broadcast_to(lax.rsqrt(mean + 1e-05), (SPAN, 128))

        def norm_step(p, _, rows=rows, inverse=inverse):
            ln = lanes_of(p)
            ob[rows, ln] = (ins[rows, ln] * inverse * gain[pl.ds(p, 1), :]).astype(BF16)
            return 0

        lax.fori_loop(0, PAIRS, norm_step, 0)

    for n in (1, 2):
        stage_arrive(n, 2)
        p_copy(3 + n, False).start()
    for j in (1, 3):
        pass_on(j, True).wait_recv()
    p_copy(2, False).start()
    held_copy.wait()
    for n in range(3):
        for stage in range(3):
            for j in (1, 3) if (n, stage) == (0, 2) else (1, 2, 3):
                stage_copy(n, stage, j, False).wait_send()
    for j in (1, 3):
        pass_on(j, False).wait_send()
    for i in range(6):
        p_copy(i, False).wait_send()
        p_copy(i, True).wait_recv()

    def drain(p, _):
        partner_copy(p).wait_send()
        entry_to_partner(p).wait_send()

        @pl.when(p != c)
        def _():
            owner_copy(p).wait_send()
            entry_copy(p).wait_send()

        return 0

    lax.fori_loop(0, PAIRS, drain, 0)


def run_mixer(values, gate, input_map, output_map, rates, steps, skip, gain, cache):
    vm = lambda *shape: pltpu.VMEM(shape, F32)
    dma = lambda *shape: pltpu.SemaphoreType.DMA(shape)
    any_spec = pl.BlockSpec(memory_space=pl.ANY)
    vmem_spec = pl.BlockSpec(memory_space=pltpu.VMEM)
    return pl.pallas_call(
        mixer_kernel,
        out_shape=(
            pltpu.VMEM((TOKENS, WIDE), BF16),
            pltpu.VMEM((GROUPS, 4, 4, 128, STATE), BF16),
            jax.ShapeDtypeStruct((2, GROUPS, 4, 4, CUT_B, HALF), BF16),
            jax.ShapeDtypeStruct((2, GROUPS, 4, 4, CUT_C - CUT_B, HALF), BF16),
            jax.ShapeDtypeStruct((2, GROUPS, 4, 4, 128 - CUT_C, HALF), BF16),
        ),
        in_specs=[any_spec, any_spec] + [vmem_spec] * 4 + [pl.BlockSpec(memory_space=pltpu.SMEM), vmem_spec, any_spec],
        out_specs=(vmem_spec, vmem_spec) + (any_spec,) * 3,
        scratch_shapes=[
            pltpu.VMEM((TOKENS, WIDE), BF16),
            pltpu.VMEM((TOKENS, WIDE), BF16),
            vm(BLOCKS - 1, STATE, WIDE),
            vm(TOKENS, WIDE),
            vm(TOKENS, WIDE),
            vm(PAIRS, 2, ROWS, 128),
            vm(PAIRS, ROWS, 128),
            vm(PAIRS, ROWS, 128),
            vm(CHIPS, ROWS, 128),
            vm(CHIPS, HALF, 128),
            vm(PAIRS, HALF, 128),
            vm(PAIRS, HALF, 128),
            vm(PAIRS, HALF, 128),
            vm(STATE, WIDE),
            vm(BLOCKS, STATE, SPAN),
            vm(BLOCKS, SPAN, SPAN),
            pltpu.VMEM((TOKENS, 128), BF16),
            vm(2, TOKENS, 256),
            pltpu.VMEM((2, BLOCKS, 256, 128), BF16),
            pltpu.VMEM((2, BLOCKS, 256, 256), BF16),
            vm(LOCAL_HEADS, TOKENS),
            vm(LOCAL_HEADS, TOKENS),
            vm(LOCAL_HEADS, TOKENS),
            vm(LOCAL_HEADS, 128),
            vm(BLOCKS, PAIRS, 128),
            vm(PAIRS, 128),
            vm(TOKENS, 128),
            pltpu.VMEM((128, HALF), BF16),
            dma(PAIRS), pltpu.SemaphoreType.DMA,
            dma(PAIRS), dma(PAIRS),
            dma(PAIRS), dma(PAIRS),
            dma(PAIRS), dma(PAIRS),
            dma(PAIRS), dma(PAIRS),
            dma(3),
            dma(3, 3), dma(3, 3), dma(3, 3), dma(3, 3), dma(3, 3), dma(3, 3), dma(2), dma(2), dma(6), dma(6),
            pltpu.SemaphoreType.DMA,
        ],
        compiler_params=pltpu.CompilerParams(
            collective_id=0, has_side_effects=True, vmem_limit_bytes=54 * 1024 * 1024
        ),
        cost_estimate=pl.CostEstimate(flops=6_000_000_000, bytes_accessed=24_000_000, transcendentals=12_000_000),
        name="mixer",
    )(values, gate, input_map, output_map, rates, steps, skip, gain, cache)


def place_kernel(slot_map, held, rows_in, ga, gb, gc, out, rows_out, buf, hin, cout, rout):
    rank = lax.axis_index("seq") * GROUPS + lax.axis_index("head")

    def final_in(g):
        for h in range(2):
            for n, (part, start, stop) in enumerate(
                ((ga, 0, CUT_B), (gb, CUT_B, CUT_C), (gc, CUT_C, 128))
            ):
                yield pltpu.make_async_copy(
                    part.at[h, g],
                    buf.at[g, :, :, pl.ds(start, stop - start), pl.ds(h * HALF, HALF)],
                    hin.at[g, 3 * h + n],
                )

    def rows_copy(b):
        rows = pl.ds(b * SPAN, SPAN)
        return pltpu.make_async_copy(rows_in.at[rows], rows_out.at[rows], rout.at[b])

    for g in range(GROUPS):
        hit = slot_map[g] == rank

        @pl.when(hit)
        def _(g=g):
            for copy in final_in(g):
                copy.start()

        @pl.when(jnp.logical_not(hit))
        def _(g=g):
            pltpu.make_async_copy(held.at[g], out.at[g], cout.at[g]).start()

        rows_copy(g).start()

    for g in range(GROUPS):
        hit = slot_map[g] == rank

        @pl.when(hit)
        def _(g=g):
            for copy in final_in(g):
                copy.wait()
            pltpu.make_async_copy(buf.at[g], out.at[g], cout.at[g]).start()

    for g in range(GROUPS):
        pltpu.make_async_copy(held.at[g], out.at[g], cout.at[g]).wait()
        rows_copy(g).wait()


def run_place(slot_map, held, rows, ga, gb, gc):
    any_spec = pl.BlockSpec(memory_space=pl.ANY)
    vmem_spec = pl.BlockSpec(memory_space=pltpu.VMEM)
    return pl.pallas_call(
        place_kernel,
        out_shape=(
            jax.ShapeDtypeStruct((GROUPS, 4, 4, 128, STATE), BF16),
            jax.ShapeDtypeStruct((TOKENS, WIDE), BF16),
        ),
        in_specs=[pl.BlockSpec(memory_space=pltpu.SMEM), vmem_spec, vmem_spec] + [any_spec] * 3,
        out_specs=(any_spec, any_spec),
        scratch_shapes=[
            pltpu.VMEM((GROUPS, 4, 4, 128, STATE), BF16),
            pltpu.SemaphoreType.DMA((GROUPS, 6)),
            pltpu.SemaphoreType.DMA((GROUPS,)),
            pltpu.SemaphoreType.DMA((GROUPS,)),
        ],
        compiler_params=pltpu.CompilerParams(vmem_limit_bytes=16 * 1024 * 1024),
        name="place",
    )(slot_map, held, rows, ga, gb, gc)


def shards(
    values, gate_rows, input_map, output_map, decay_rate, step_size, skip_gain, norm_gain, slot_map, state_cache
):
    gain = norm_gain.reshape(PAIRS, 128)
    cache = state_cache.reshape(GROUPS, 4, 4, 128, STATE)
    rows, held, ga, gb, gc = run_mixer(
        values, gate_rows, input_map, output_map, decay_rate.T, step_size.T, skip_gain, gain, cache
    )
    held, rows = (pltpu.with_memory_space_constraint(a, pltpu.VMEM) for a in (held, rows))
    ga, gb, gc = (pltpu.with_memory_space_constraint(a, pltpu.HBM) for a in (ga, gb, gc))
    new_cache, mixed_rows = run_place(slot_map, held, rows, ga, gb, gc)
    return mixed_rows, new_cache.reshape(state_cache.shape)


def solution(mesh):
    return jax.shard_map(
        shards,
        mesh=mesh,
        in_specs=(
            P("seq", "head"),
            P("seq", "head"),
            P("seq", "head"),
            P("seq", "head"),
            P("seq", "head"),
            P("seq", "head"),
            P("head"),
            P("head"),
            P(),
            P(("seq", "head"), None, None, None),
        ),
        out_specs=(P("seq", "head"), P(("seq", "head"), None, None, None)),
        check_vma=False,
    )
```

time: 89.2 us -> 69.1 us (0.77)
  Pallas kernels: 88.4 us -> 68.2 us
    pallas_call x2, Pallas kernels: 88.4 us -> 68.2 us  [the longest x1 64.1 us: run_mixer(): pl.pallas_call(mixer_kernel, out_shape=(pltpu.VMEM((TOKENS, WIDE), BF16),...]
where the time goes in v2:
time: 69.1 us; the launch traced here: 68.9 us
  Pallas kernels  68.2 us (99%)
    pallas_call x1, Pallas kernels, run_mixer(): pl.pallas_call(mixer_kernel, out_shape=(pltpu.VMEM((TOKENS, WIDE), BF16),...  64.1 us
    pallas_call x1, Pallas kernels, run_place(): pl.pallas_call(place_kernel, out_shape=(jax.ShapeDtypeStruct((GROUPS, 4,...  4.16 us

profile of v2, /device:TPU:1, one launch (start us, length us, event | category | flops | bytes accessed | tf_op | source)
XLA Modules:
  0.0 68.9 jit_solution(6952335944590326959)
XLA Ops:
  0.6 0.0 copy-start
  0.6 64.1 %mixer.1 = (bf16[1024,2048]{1,0:T(8,128)(2,1)S(1)}, bf16[4,4,4,128,256]{4,3,2,1,0:T(8,128)(2,1)S(1)}, bf16[2,4,4,4,96,128]{5,4,3,2,1,0:T(8,128)(2,1)}, bf16[2,4,...) custom-call(bf16[1024,2048]{1,0:T(8,128)(2,1)} %values.1, bf16[1024,2048]{1,0:T(8,128)(2,1)} %gate.1, ...), custom_call_target="tpu_custom_call" | custom-call | flops 6000000000 | bytes 24000000 | tf_op jit(solution)/shard_map/mixer/pallas_call | solution.py:498
  64.7 0.0 copy-done
  64.8 4.2 %place.1 = (bf16[4,4,4,128,256]{4,3,2,1,0:T(8,128)(2,1)}, bf16[1024,2048]{1,0:T(8,128)(2,1)}) custom-call(s32[4]{0:T(128)S(1)} %copy-done, bf16[4,4,4,128,256]{4,3,2,1,0:T(8,128)(2,1)S(1)} %get-tuple-element.9.held, bf16[1024,2048]{1,0:T(8,128)(2,1)S(1)} %get-tuple-element.10.rows_in, bf16[2,4,4,4,96,128]{5,4,3,2,1,0:T(8,128)(2,1)} %get-tuple-element.11.ga, ...), custom_call_target="tpu_custom_call" | custom-call | tf_op jit(solution)/shard_map/place/pallas_call | solution.py:604
Async XLA Ops:
  0.6 64.1 %copy-start = (s32[4]{0:T(128)S(1)}, s32[4]{0:T(128)}, u32[]{:S(2)}) copy-start(s32[4]{0:T(128)} %slot_map.1) | copy-start | bytes 52

commit v3 on v2

--- a/solution.py
+++ b/solution.py
@@ -27,10 +27,11 @@
 LOG2E = 1.4426950408889634
 LAG = 3
 TOP = 127.9999
-EARLY = 4
+EARLY = 7
+AHEAD = 6
 MIDDLE = 1
 SWITCH = 3
-PASS = 14
+PASS = 5
 CUT_B, CUT_C = 96, 112
 
 
@@ -61,7 +62,7 @@
     xv, zv, adds, ins, fac, sbuf, prt, cbuf, own_in, ebuf, ent_in, mbuf, pin, entry,
     bt, ip, rcol, minus, wtop, wlow, run_t, step_t, trail_t, dwide, dec, ddec, sq, fin,
     xsem, zsem, ps_s, ps_r, os_s, os_r, en_s, en_r, ms_s, ms_r,
-    gl_s, g1_s, g1_r, g2_s, g2_r, g3_s, g3_r, gh_s, gh_r, gp_s, gp_r, held_sem,
+    gl_s, g1_s, g1_r, g2_s, g2_r, g3_s, g3_r, gy_s, gy_r, gd_s, gd_r, gp_s, gp_r, held_sem,
 ):
     seq = lax.axis_index("seq")
     y = lax.axis_index("head")
@@ -79,6 +80,14 @@
 
     first = k == 0
 
+    def x_copy(p):
+        return pltpu.make_async_copy(values.at[:, lanes_of(p)], xv.at[:, lanes_of(p)], xsem.at[p])
+
+    def start_x(i, _):
+        x_copy(served(i)).start()
+        return 0
+
+    lax.fori_loop(0, PAIRS, start_x, 0)
     barrier = pltpu.get_barrier_semaphore()
     pl.semaphore_signal(barrier, inc=1, device_id={"seq": partner}, device_id_type=MESH)
 
@@ -93,18 +102,8 @@
             barrier, inc=1, device_id={"head": lax.rem(y + j, GROUPS)}, device_id_type=MESH
         )
 
-    def x_copy(p):
-        return pltpu.make_async_copy(values.at[:, lanes_of(p)], xv.at[:, lanes_of(p)], xsem.at[p])
-
-    def start_x(i, _):
-        x_copy(served(i)).start()
-        return 0
-
-    lax.fori_loop(0, PAIRS, start_x, 0)
     z_copy = pltpu.make_async_copy(gate, zv, zsem)
-    z_copy.start()
     held_copy = pltpu.make_async_copy(cache, held, held_sem)
-    held_copy.start()
 
     lane = lax.broadcasted_iota(jnp.int32, (SPAN, 128), 1)
     low = lane < 64
@@ -214,6 +213,8 @@
         return 0
 
     lax.fori_loop(0, PAIRS // 2, states_step, 0)
+    z_copy.start()
+    held_copy.start()
     send_owner(served(PAIRS - 2))
     both, decay = combine(c)
     own_in[c, 0:HALF, :] = both
@@ -286,7 +287,7 @@
     fin[...] = last.T.astype(BF16)
 
     rows_a, rows_b, rows_c = pl.ds(0, CUT_B), pl.ds(CUT_B, CUT_C - CUT_B), pl.ds(CUT_C, 128 - CUT_C)
-    parts = ((rows_a, ga, "zxy"), (rows_b, gb, "yzx"), (rows_c, gc, "yxz"))
+    parts = ((rows_a, ga, "xzy"), (rows_b, gb, "yzx"), (rows_c, gc, "yxz"))
 
     def keep(n):
         rows, g, _ = parts[n]
@@ -325,19 +326,51 @@
         for j in (1, 3, 2):
             stage_copy(n, stage, j, True).wait_recv()
 
-    def pass_on(j, arrival):
-        half = pl.ds(0, 2) if j == 1 else pl.ds(2, 2)
-        at = lax.rem(y + (2 if arrival else 4 - j), 4)
-        part = ga.at[k, at, half]
-        return pltpu.make_async_remote_copy(
-            src_ref=part, dst_ref=part, send_sem=gh_s.at[j // 2], recv_sem=gh_r.at[j // 2],
+    def y_copy(r, j, arrival):
+        there = ga.at[k, lax.rem(y + 4 - j, 4) if arrival else y, lax.rem(xc + 4 - r, 4)]
+        return pltpu.make_async_remote_copy(
+            src_ref=there, dst_ref=there, send_sem=gy_s.at[r, j - 1], recv_sem=gy_r.at[r, j - 1],
             device_id=peer("y", j), device_id_type=MESH,
         )
+
+    def plane_copy(d):
+        return pltpu.make_async_remote_copy(
+            src_ref=fin.at[rows_a], dst_ref=ga.at[k, y, xc, zc], send_sem=gd_s.at[d], recv_sem=gd_r.at[c],
+            device_id={"seq": 2 * d + k}, device_id_type=MESH,
+        )
+
+    def plane_arrival(d):
+        return pltpu.make_async_remote_copy(
+            src_ref=fin.at[rows_a], dst_ref=ga.at[k, y, d // 4, lax.rem(d, 4)],
+            send_sem=gd_s.at[d], recv_sem=gd_r.at[d],
+            device_id={"seq": 2 * d + k}, device_id_type=MESH,
+        )
+
+    def plane_send(i, _):
+        plane_copy(served(i)).start()
+        return 0
+
+    def row_arrive(r):
+        def step(i, _):
+            d = lax.rem(xc + 4 - r, 4) * 4 + i
+
+            @pl.when(d != c)
+            def _():
+                plane_arrival(d).wait_recv()
+
+            return 0
+
+        lax.fori_loop(0, 4, step, 0)
+
+    def y_send(r):
+        for j in (1, 3, 2):
+            y_copy(r, j, False).start()
 
     for n in range(3):
         keep(n).start()
-    for n in range(3):
+    for n in (1, 2):
         stage_send(n, 0)
+    lax.fori_loop(0, CHIPS - 1, plane_send, 0)
 
     def entry_copy(j):
         return pltpu.make_async_remote_copy(
@@ -355,12 +388,15 @@
         entry_copy(served(i)).start()
         return 0
 
+    lax.fori_loop(0, AHEAD, send_entry, 0)
     lax.fori_loop(EARLY, EARLY + MIDDLE, inner, 0)
     for n in range(3):
         keep(n).wait()
+    for n in (1, 2):
         stage_arrive(n, 0)
         stage_send(n, 1)
-    lax.fori_loop(0, CHIPS - 1, send_entry, 0)
+    row_arrive(0)
+    y_send(0)
     ent_in[c] = ebuf[c]
 
     lax.fori_loop(EARLY + MIDDLE, PAIRS // 2, inner, 0)
@@ -411,6 +447,10 @@
         def _():
             receive(serving(lax.rem(i + PAIRS - 1, PAIRS)))
 
+        @pl.when(i + AHEAD < CHIPS - 1)
+        def _():
+            send_entry(i + AHEAD, 0)
+
         @pl.when(i >= LAG)
         def _():
             finish(serving(lax.rem(i + PAIRS - 1 - LAG, PAIRS)))
@@ -433,18 +473,16 @@
         )
 
     lax.fori_loop(0, SWITCH, finish_step, 0)
-    stage_arrive(0, 1)
     for j in (1, 3):
-        stage_copy(0, 2, j, False).start()
+        row_arrive(j)
+        y_send(j)
+    lax.fori_loop(SWITCH, PASS, finish_step, 0)
+    row_arrive(2)
+    y_send(2)
+    p_copy(0, False).start()
     for n in (1, 2):
         stage_arrive(n, 1)
         stage_send(n, 2)
-    p_copy(0, False).start()
-    lax.fori_loop(SWITCH, PASS, finish_step, 0)
-    for j in (1, 3):
-        stage_copy(0, 2, j, True).wait_recv()
-        pass_on(j, False).start()
-        p_copy(j, False).start()
     lax.fori_loop(PASS, PAIRS + LAG, finish_step, 0)
 
     for b in range(BLOCKS):
@@ -462,16 +500,18 @@
     for n in (1, 2):
         stage_arrive(n, 2)
         p_copy(3 + n, False).start()
-    for j in (1, 3):
-        pass_on(j, True).wait_recv()
-    p_copy(2, False).start()
+    for j in (1, 3, 2):
+        for r in range(4):
+            y_copy(r, j, True).wait_recv()
+        p_copy(j, False).start()
     held_copy.wait()
-    for n in range(3):
+    for n in (1, 2):
         for stage in range(3):
-            for j in (1, 3) if (n, stage) == (0, 2) else (1, 2, 3):
+            for j in range(1, 4):
                 stage_copy(n, stage, j, False).wait_send()
-    for j in (1, 3):
-        pass_on(j, False).wait_send()
+    for r in range(4):
+        for j in range(1, 4):
+            y_copy(r, j, False).wait_send()
     for i in range(6):
         p_copy(i, False).wait_send()
         p_copy(i, True).wait_recv()
@@ -484,6 +524,7 @@
         def _():
             owner_copy(p).wait_send()
             entry_copy(p).wait_send()
+            plane_copy(p).wait_send()
 
         return 0
 
@@ -541,7 +582,7 @@
             dma(PAIRS), dma(PAIRS),
             dma(PAIRS), dma(PAIRS),
             dma(3),
-            dma(3, 3), dma(3, 3), dma(3, 3), dma(3, 3), dma(3, 3), dma(3, 3), dma(2), dma(2), dma(6), dma(6),
+            dma(3, 3), dma(3, 3), dma(3, 3), dma(3, 3), dma(3, 3), dma(3, 3), dma(4, 3), dma(4, 3), dma(CHIPS), dma(CHIPS), dma(6), dma(6),
             pltpu.SemaphoreType.DMA,
         ],
         compiler_params=pltpu.CompilerParams(

time: 69.1 us -> 66.8 us (0.967)
  Pallas kernels: 68.2 us -> 66 us
    pallas_call x1, Pallas kernels: 64.1 us -> 61.8 us  [run_mixer(): pl.pallas_call(mixer_kernel, out_shape=(pltpu.VMEM((TOKENS, WIDE), BF16),...]
where the time goes in v3:
time: 66.8 us; the launch traced here: 66.7 us
  Pallas kernels  66 us (99%)
    pallas_call x1, Pallas kernels, run_mixer(): pl.pallas_call(mixer_kernel, out_shape=(pltpu.VMEM((TOKENS, WIDE), BF16),...  61.8 us
    pallas_call x1, Pallas kernels, run_place(): pl.pallas_call(place_kernel, out_shape=(jax.ShapeDtypeStruct((GROUPS, 4,...  4.16 us

profile of v3, /device:TPU:1, one launch (start us, length us, event | category | flops | bytes accessed | tf_op | source)
XLA Modules:
  0.0 66.7 jit_solution(12295601967895936149)
XLA Ops:
  0.6 0.0 copy-start
  0.6 61.8 %mixer.1 = (bf16[1024,2048]{1,0:T(8,128)(2,1)S(1)}, bf16[4,4,4,128,256]{4,3,2,1,0:T(8,128)(2,1)S(1)}, bf16[2,4,4,4,96,128]{5,4,3,2,1,0:T(8,128)(2,1)}, bf16[2,4,...) custom-call(bf16[1024,2048]{1,0:T(8,128)(2,1)} %values.1, bf16[1024,2048]{1,0:T(8,128)(2,1)} %gate.1, ...), custom_call_target="tpu_custom_call" | custom-call | flops 6000000000 | bytes 24000000 | tf_op jit(solution)/shard_map/mixer/pallas_call | solution.py:539
  62.5 0.0 copy-done
  62.5 4.2 %place.1 = (bf16[4,4,4,128,256]{4,3,2,1,0:T(8,128)(2,1)}, bf16[1024,2048]{1,0:T(8,128)(2,1)}) custom-call(s32[4]{0:T(128)S(1)} %copy-done, bf16[4,4,4,128,256]{4,3,2,1,0:T(8,128)(2,1)S(1)} %get-tuple-element.9.held, bf16[1024,2048]{1,0:T(8,128)(2,1)S(1)} %get-tuple-element.10.rows_in, bf16[2,4,4,4,96,128]{5,4,3,2,1,0:T(8,128)(2,1)} %get-tuple-element.11.ga, ...), custom_call_target="tpu_custom_call" | custom-call | tf_op jit(solution)/shard_map/place/pallas_call | solution.py:645
Async XLA Ops:
  0.6 61.9 %copy-start = (s32[4]{0:T(128)S(1)}, s32[4]{0:T(128)}, u32[]{:S(2)}) copy-start(s32[4]{0:T(128)} %slot_map.1) | copy-start | bytes 52

commit v4 on v3

--- a/solution.py
+++ b/solution.py
@@ -30,8 +30,7 @@
 EARLY = 7
 AHEAD = 6
 MIDDLE = 1
-SWITCH = 3
-PASS = 5
+STOPS = (3, 4, 5, 8)
 CUT_B, CUT_C = 96, 112
 
 
@@ -472,18 +471,18 @@
             device_id={"seq": partner}, device_id_type=MESH,
         )
 
-    lax.fori_loop(0, SWITCH, finish_step, 0)
-    for j in (1, 3):
-        row_arrive(j)
-        y_send(j)
-    lax.fori_loop(SWITCH, PASS, finish_step, 0)
-    row_arrive(2)
-    y_send(2)
+    done = 0
+    for n, r in enumerate((1, 3, 2)):
+        lax.fori_loop(done, STOPS[n], finish_step, 0)
+        done = STOPS[n]
+        row_arrive(r)
+        y_send(r)
     p_copy(0, False).start()
+    lax.fori_loop(done, STOPS[3], finish_step, 0)
     for n in (1, 2):
         stage_arrive(n, 1)
         stage_send(n, 2)
-    lax.fori_loop(PASS, PAIRS + LAG, finish_step, 0)
+    lax.fori_loop(STOPS[3], PAIRS + LAG, finish_step, 0)
 
     for b in range(BLOCKS):
         rows = slice(b * SPAN, (b + 1) * SPAN)

time: 66.8 us -> 66.4 us (level)
  no operation moved by 1% of the time
where the time goes in v4:
time: 66.4 us; the launch traced here: 66.3 us
  Pallas kernels  65.6 us (99%)
    pallas_call x1, Pallas kernels, run_mixer(): pl.pallas_call(mixer_kernel, out_shape=(pltpu.VMEM((TOKENS, WIDE), BF16),...  61.4 us
    pallas_call x1, Pallas kernels, run_place(): pl.pallas_call(place_kernel, out_shape=(jax.ShapeDtypeStruct((GROUPS, 4,...  4.16 us

profile of v4, /device:TPU:1, one launch (start us, length us, event | category | flops | bytes accessed | tf_op | source)
XLA Modules:
  0.0 66.3 jit_solution(1505362361737162227)
XLA Ops:
  0.6 0.0 copy-start
  0.6 61.4 %mixer.1 = (bf16[1024,2048]{1,0:T(8,128)(2,1)S(1)}, bf16[4,4,4,128,256]{4,3,2,1,0:T(8,128)(2,1)S(1)}, bf16[2,4,4,4,96,128]{5,4,3,2,1,0:T(8,128)(2,1)}, bf16[2,4,...) custom-call(bf16[1024,2048]{1,0:T(8,128)(2,1)} %values.1, bf16[1024,2048]{1,0:T(8,128)(2,1)} %gate.1, ...), custom_call_target="tpu_custom_call" | custom-call | flops 6000000000 | bytes 24000000 | tf_op jit(solution)/shard_map/mixer/pallas_call | solution.py:538
  62.1 0.0 copy-done
  62.1 4.2 %place.1 = (bf16[4,4,4,128,256]{4,3,2,1,0:T(8,128)(2,1)}, bf16[1024,2048]{1,0:T(8,128)(2,1)}) custom-call(s32[4]{0:T(128)S(1)} %copy-done, bf16[4,4,4,128,256]{4,3,2,1,0:T(8,128)(2,1)S(1)} %get-tuple-element.9.held, bf16[1024,2048]{1,0:T(8,128)(2,1)S(1)} %get-tuple-element.10.rows_in, bf16[2,4,4,4,96,128]{5,4,3,2,1,0:T(8,128)(2,1)} %get-tuple-element.11.ga, ...), custom_call_target="tpu_custom_call" | custom-call | tf_op jit(solution)/shard_map/place/pallas_call | solution.py:644
Async XLA Ops:
  0.6 61.5 %copy-start = (s32[4]{0:T(128)S(1)}, s32[4]{0:T(128)}, u32[]{:S(2)}) copy-start(s32[4]{0:T(128)} %slot_map.1) | copy-start | bytes 52
